TPU v7x, 128 devices: a whole 4x4x4 slice. The times are simulated.
128 devices in a mesh: shard: 16 (over z, x), rep: 8 (over y, core).
Axes of the slice: x: 4, y: 4, z: 4, core: 2. Of those that a mesh axis runs over, the one named last changes fastest.
Arguments:
- embeddings: bfloat16 [256, 512, 768], P('shard'), may hold values from -8.375 to 8.375
- labels: bfloat16 [256, 1000, 512], P('shard', 'rep'), may hold values from -30 to 30
- block_pairs: int32 [640, 2], replicated, may hold values from 0 to 255, as said below
- block_slot: int32 [256], replicated, may hold values from 0 to 255, as said below
Outputs:
- propagated: float32 [256, 1000, 512], P('shard', 'rep')
Inputs may be any that keep to these rules, and one draw needn't show every extreme that they name: `block_slot`: blocks 16 * g to 16 * g + 15 form cluster g; they lie in the slots o * 16 + g, one for each o in 0 to 15, in an order drawn from the seed. Every slot is used once. `block_pairs`: rows 40 * g to 40 * g + 39 join two different blocks of cluster g, the first number smaller; no pair appears twice; every block is in some pair.
All inputs are finite; a program needn't handle non-finite values.
Results may differ from a plain program's by a relative error of at most 0.0065.
Values may be sent and summed in bfloat16 or wider, within the bound.
A program may use at most 256 MiB of HBM per device.

v0:
```python
import math

import jax
import jax.numpy as jnp
from jax import lax
from jax.sharding import PartitionSpec as P

ITERS = 2


ALPHA = 0.9


def cluster_pairs(block_pairs, block_slot):
    owners = lax.axis_size("shard")
    pair_count = block_pairs.shape[0] // owners
    own_pairs = lax.dynamic_slice_in_dim(
        block_pairs, lax.axis_index("shard") * pair_count, pair_count, 0
    )
    owner_of = block_slot // owners
    first_idx = jnp.take(owner_of, own_pairs[:, 0])
    second_idx = jnp.take(owner_of, own_pairs[:, 1])
    return (first_idx, second_idx)


def build_kernel(cluster_emb, first_idx, second_idx):
    members = cluster_emb.shape[0]
    kernel_scale = 1.0 / math.sqrt(cluster_emb.shape[2])
    left_sets = first_idx.reshape(4, -1)
    right_sets = second_idx.reshape(4, -1)

    def one_batch(indices):
        left_idx, right_idx = indices
        rows_a = jnp.take(cluster_emb, left_idx, axis=0)
        rows_b = jnp.take(cluster_emb, right_idx, axis=0)
        scores = jnp.einsum("pid,pjd->pij", rows_a, rows_b, preferred_element_type=jnp.float32)
        kernel = jnp.exp(scores * kernel_scale)
        return (kernel.astype(jnp.bfloat16), jnp.sum(kernel, axis=2), jnp.sum(kernel, axis=1))

    kernel_tiles, row_sums, col_sums = lax.map(one_batch, (left_sets, right_sets))
    pair_count = first_idx.shape[0]
    kernel_tiles = kernel_tiles.reshape((pair_count,) + kernel_tiles.shape[2:])
    row_sums = row_sums.reshape(pair_count, -1)
    col_sums = col_sums.reshape(pair_count, -1)
    member_ids = jnp.arange(members, dtype=jnp.int32)[None, :]
    onehot_a = (first_idx[:, None] == member_ids).astype(jnp.float32)
    onehot_b = (second_idx[:, None] == member_ids).astype(jnp.float32)
    degree = jnp.einsum("pk,px->kx", onehot_a, row_sums, precision=lax.Precision.HIGHEST)
    degree = degree + jnp.einsum("pk,px->kx", onehot_b, col_sums, precision=lax.Precision.HIGHEST)
    return (kernel_tiles, degree, onehot_a, onehot_b)


def propagate(kernel_tiles, first_idx, second_idx, onehot_a, onehot_b, outgoing):
    labels_a = jnp.take(outgoing, first_idx, axis=0)
    labels_b = jnp.take(outgoing, second_idx, axis=0)
    to_first = jnp.einsum(
        "pcj,pij->pci", labels_b, kernel_tiles, preferred_element_type=jnp.float32
    )
    to_second = jnp.einsum(
        "pci,pij->pcj", labels_a, kernel_tiles, preferred_element_type=jnp.float32
    )
    summed = jnp.einsum("pk,pcx->kcx", onehot_a, to_first, precision=lax.Precision.HIGHEST)
    return summed + jnp.einsum("pk,pcx->kcx", onehot_b, to_second, precision=lax.Precision.HIGHEST)


def body(embeddings, labels, block_pairs, block_slot):
    first_idx, second_idx = cluster_pairs(block_pairs, block_slot)
    cluster_emb = lax.all_to_all(embeddings, "shard", split_axis=0, concat_axis=0, tiled=True)
    kernel_tiles, degree, onehot_a, onehot_b = build_kernel(cluster_emb, first_idx, second_idx)
    own_degree = lax.all_to_all(degree, "shard", split_axis=0, concat_axis=0, tiled=True)
    scaling = (1.0 / jnp.sqrt(own_degree))[:, None, :]
    seed_labels = labels.astype(jnp.float32)
    label_field = seed_labels
    for iteration in range(ITERS):
        outgoing = (label_field * scaling).astype(jnp.bfloat16)
        gathered = lax.all_to_all(outgoing, "shard", split_axis=0, concat_axis=0, tiled=True)
        products = propagate(kernel_tiles, first_idx, second_idx, onehot_a, onehot_b, gathered)
        returned = lax.all_to_all(products, "shard", split_axis=0, concat_axis=0, tiled=True)
        label_field = ALPHA * scaling * returned + (1.0 - ALPHA) * seed_labels
    return label_field


def solution(mesh):
    return jax.shard_map(
        body,
        mesh=mesh,
        in_specs=(P("shard", None, None), P("shard", "rep", None), P(), P()),
        out_specs=P("shard", "rep", None),
        check_vma=False,
    )
```

profile of v0, /device:TPU:0, one launch (start us, length us, event | category | flops | bytes accessed | tf_op | source)
XLA Modules:
  0.0 699.4 jit_solution(18223447448332884356)
XLA Ops:
  0.0 8.1 %all-to-all-start = ((bf16[16,512,768]{2,1,0:T(8,128)(2,1)}), bf16[16,512,768]{2,1,0:T(8,128)(2,1)}, u32[]{:S(2)}, u32[]{:S(2)}) async-start(bf16[16,512,768]{2,1,0:T(8,128)(2,1)} %param.12), calls=%async_computation | async-start | bytes 25165824 | tf_op jit(solution)/shard_map/all_to_all | solution.py:68
  10.6 184.4 %all-to-all-done = bf16[16,512,768]{2,1,0:T(8,128)(2,1)} async-done(((bf16[16,512,768]{2,1,0:T(8,128)(2,1)}), bf16[16,512,768]{2,1,0:T(8,128)(2,1)}, u32[]{:S(2)}, u32[]{:S(2)}) %all-to-all-start) | async-done | bytes 12582944 | tf_op jit(solution)/shard_map/all_to_all | solution.py:68
  195.0 164.0 %while.14 = (s32[]{:T(128)}, bf16[4,10,512,512]{3,2,1,0:T(8,128)(2,1)}, f32[4,10,512]{2,1,0:T(8,128)S(1)}, f32[4,10,512]{2,1,0:T(8,128)S(1)}, s32[4,10]{1,0:T(4,...) while((s32[]{:T(128)}, bf16[4,10,512,512]{3,2,1,0:T(8,128)(2,1)}, ...), condition=%wide.region_3.6_spmd, body=%wide.region_0.5_spmd.sunk | while | flops 4047495168 | bytes 73581512 | solution.py:40
  195.0 9.8 %gather_fusion = bf16[10,512,768]{2,1,0:T(8,128)(2,1)} fusion(bf16[16,512,768]{2,1,0:T(8,128)(2,1)} %get-tuple-element.170, s32[1024]{0:T(1024)S(1)} %pad_clamp_fusion.8), kind=kCustom, calls=%fused_computation.4.clone.clone.1 | custom fusion | bytes 15728680 | tf_op jit(solution)/shard_map/while/body/eval_jaxpr/jit(_take)/gather | solution.py:35
  204.8 9.7 %gather_fusion.1 = bf16[10,512,768]{2,1,0:T(8,128)(2,1)} fusion(bf16[16,512,768]{2,1,0:T(8,128)(2,1)} %get-tuple-element.170, s32[1024]{0:T(1024)S(1)} %pad_clamp_fusion.9), kind=kCustom, calls=%fused_computation.1.clone.clone.1 | custom fusion | bytes 15728680 | tf_op jit(solution)/shard_map/while/body/eval_jaxpr/jit(_take)/gather | solution.py:34
  214.5 15.7 %fusion.75 = (bf16[4,10,512,512]{3,2,1,0:T(8,128)(2,1)}, f32[10,512,512]{2,1,0:T(8,128)}) fusion(bf16[4,10,512,512]{3,2,1,0:T(8,128)(2,1)} %get-tuple-element.158, s32[]{:T(128)} %get-tuple-element.157, bf16[10,512,768]{2,1,0:T(8,128)(2,1)} %gather_fusion, pred[10]{0:T(512)(128)(4,1)S(1)} %get-tuple-element.140, ...), kind=kOutput, calls=%fused_computation.18.clone.1 | convolution fusion | flops 4039639040 | bytes 31457812 | tf_op jit(solution)/shard_map/while/body/eval_jaxpr/pid,pjd->pij/dot_general | solution.py:36
  230.2 5.8 fusion.76
  236.1 9.6 %gather_fusion = bf16[10,512,768]{2,1,0:T(8,128)(2,1)} fusion(bf16[16,512,768]{2,1,0:T(8,128)(2,1)} %get-tuple-element.170, s32[1024]{0:T(1024)S(1)} %pad_clamp_fusion.8), kind=kCustom, calls=%fused_computation.4.clone.clone.1 | custom fusion | bytes 15728680 | tf_op jit(solution)/shard_map/while/body/eval_jaxpr/jit(_take)/gather | solution.py:35
  245.7 9.6 %gather_fusion.1 = bf16[10,512,768]{2,1,0:T(8,128)(2,1)} fusion(bf16[16,512,768]{2,1,0:T(8,128)(2,1)} %get-tuple-element.170, s32[1024]{0:T(1024)S(1)} %pad_clamp_fusion.9), kind=kCustom, calls=%fused_computation.1.clone.clone.1 | custom fusion | bytes 15728680 | tf_op jit(solution)/shard_map/while/body/eval_jaxpr/jit(_take)/gather | solution.py:34
  255.3 15.8 %fusion.75 = (bf16[4,10,512,512]{3,2,1,0:T(8,128)(2,1)}, f32[10,512,512]{2,1,0:T(8,128)}) fusion(bf16[4,10,512,512]{3,2,1,0:T(8,128)(2,1)} %get-tuple-element.158, s32[]{:T(128)} %get-tuple-element.157, bf16[10,512,768]{2,1,0:T(8,128)(2,1)} %gather_fusion, pred[10]{0:T(512)(128)(4,1)S(1)} %get-tuple-element.140, ...), kind=kOutput, calls=%fused_computation.18.clone.1 | convolution fusion | flops 4039639040 | bytes 31457812 | tf_op jit(solution)/shard_map/while/body/eval_jaxpr/pid,pjd->pij/dot_general | solution.py:36
  271.1 5.8 fusion.76
  277.0 9.7 %gather_fusion = bf16[10,512,768]{2,1,0:T(8,128)(2,1)} fusion(bf16[16,512,768]{2,1,0:T(8,128)(2,1)} %get-tuple-element.170, s32[1024]{0:T(1024)S(1)} %pad_clamp_fusion.8), kind=kCustom, calls=%fused_computation.4.clone.clone.1 | custom fusion | bytes 15728680 | tf_op jit(solution)/shard_map/while/body/eval_jaxpr/jit(_take)/gather | solution.py:35
  286.7 9.7 %gather_fusion.1 = bf16[10,512,768]{2,1,0:T(8,128)(2,1)} fusion(bf16[16,512,768]{2,1,0:T(8,128)(2,1)} %get-tuple-element.170, s32[1024]{0:T(1024)S(1)} %pad_clamp_fusion.9), kind=kCustom, calls=%fused_computation.1.clone.clone.1 | custom fusion | bytes 15728680 | tf_op jit(solution)/shard_map/while/body/eval_jaxpr/jit(_take)/gather | solution.py:34
  296.4 15.8 %fusion.75 = (bf16[4,10,512,512]{3,2,1,0:T(8,128)(2,1)}, f32[10,512,512]{2,1,0:T(8,128)}) fusion(bf16[4,10,512,512]{3,2,1,0:T(8,128)(2,1)} %get-tuple-element.158, s32[]{:T(128)} %get-tuple-element.157, bf16[10,512,768]{2,1,0:T(8,128)(2,1)} %gather_fusion, pred[10]{0:T(512)(128)(4,1)S(1)} %get-tuple-element.140, ...), kind=kOutput, calls=%fused_computation.18.clone.1 | convolution fusion | flops 4039639040 | bytes 31457812 | tf_op jit(solution)/shard_map/while/body/eval_jaxpr/pid,pjd->pij/dot_general | solution.py:36
  312.2 5.8 fusion.76
  318.1 9.6 %gather_fusion = bf16[10,512,768]{2,1,0:T(8,128)(2,1)} fusion(bf16[16,512,768]{2,1,0:T(8,128)(2,1)} %get-tuple-element.170, s32[1024]{0:T(1024)S(1)} %pad_clamp_fusion.8), kind=kCustom, calls=%fused_computation.4.clone.clone.1 | custom fusion | bytes 15728680 | tf_op jit(solution)/shard_map/while/body/eval_jaxpr/jit(_take)/gather | solution.py:35
  327.7 9.7 %gather_fusion.1 = bf16[10,512,768]{2,1,0:T(8,128)(2,1)} fusion(bf16[16,512,768]{2,1,0:T(8,128)(2,1)} %get-tuple-element.170, s32[1024]{0:T(1024)S(1)} %pad_clamp_fusion.9), kind=kCustom, calls=%fused_computation.1.clone.clone.1 | custom fusion | bytes 15728680 | tf_op jit(solution)/shard_map/while/body/eval_jaxpr/jit(_take)/gather | solution.py:34
  337.4 15.7 %fusion.75 = (bf16[4,10,512,512]{3,2,1,0:T(8,128)(2,1)}, f32[10,512,512]{2,1,0:T(8,128)}) fusion(bf16[4,10,512,512]{3,2,1,0:T(8,128)(2,1)} %get-tuple-element.158, s32[]{:T(128)} %get-tuple-element.157, bf16[10,512,768]{2,1,0:T(8,128)(2,1)} %gather_fusion, pred[10]{0:T(512)(128)(4,1)S(1)} %get-tuple-element.140, ...), kind=kOutput, calls=%fused_computation.18.clone.1 | convolution fusion | flops 4039639040 | bytes 31457812 | tf_op jit(solution)/shard_map/while/body/eval_jaxpr/pid,pjd->pij/dot_general | solution.py:36
  353.1 5.8 fusion.76
  359.4 12.0 %all_to_all.34 = f32[16,1,512]{2,1,0:T(1,128)S(1)} all-to-all(f32[16,1,512]{2,1,0:T(1,128)S(1)} %copy.9), channel_id=1, replica_groups=mesh['shard'=16,'rep'=8] {'shard'}, dimensions={0} | all-to-all | bytes 65536 | tf_op jit(solution)/shard_map/all_to_all | solution.py:70
  377.9 27.3 %all-to-all-done.2 = bf16[16,125,512]{2,1,0:T(8,128)(2,1)S(1)} async-done(((bf16[16,125,512]{2,1,0:T(8,128)(2,1)}), bf16[16,125,512]{2,1,0:T(8,128)(2,1)S(1)}, u32[]{:S(2)}, u32[]{:S(2)}) %all-to-all-start.2) | async-done | bytes 2048032 | tf_op jit(solution)/shard_map/all_to_all | solution.py:76
  410.0 15.4 %fusion.26 = f32[40,125,512]{2,1,0:T(8,128)} fusion(bf16[40,512,512]{2,1,0:T(8,128)(2,1)} %bitcast.55, bf16[40,125,512]{2,1,0:T(8,128)(2,1)} %gather_fusion.5, pred[40]{0:T(512)(128)(4,1)S(1)} %get-tuple-element.80), kind=kOutput, calls=%fused_computation.47 | convolution fusion | flops 2624000000 | bytes 36331560 | tf_op jit(solution)/shard_map/pci,pij->pcj/dot_general | solution.py:59
  425.4 15.2 %fusion.18 = f32[16,125,512]{2,0,1:T(8,128)} fusion(f32[40,125,512]{2,1,0:T(8,128)} %fusion.26, s32[40]{0:T(128)S(1)} %get-tuple-element.71), kind=kOutput, calls=%fused_computation.37 | convolution fusion | flops 491520640 | bytes 14336160 | tf_op jit(solution)/shard_map/pk,pcx->kcx/dot_general | solution.py:63
  445.2 14.4 %fusion.28 = f32[40,125,512]{2,1,0:T(8,128)} fusion(bf16[40,512,512]{2,1,0:T(8,128)(2,1)} %bitcast.56, bf16[40,125,512]{2,1,0:T(8,128)(2,1)} %gather_fusion.4, pred[40]{0:T(512)(128)(4,1)S(1)} %copy-done.6), kind=kOutput, calls=%fused_computation.49 | convolution fusion | flops 2624000000 | bytes 36331560 | tf_op jit(solution)/shard_map/pcj,pij->pci/dot_general | solution.py:56
  459.6 14.4 %fusion.43 = f32[16,125,512]{2,0,1:T(8,128)S(1)} fusion(f32[16,125,512]{2,0,1:T(8,128)} %fusion.18, f32[40,125,512]{2,1,0:T(8,128)} %fusion.28, s32[40]{0:T(128)S(1)} %get-tuple-element.81), kind=kOutput, calls=%fused_computation.64 | convolution fusion | flops 492544640 | bytes 18432160 | tf_op jit(solution)/shard_map/pk,pcx->kcx/dot_general | solution.py:62
  483.3 57.4 %all-to-all-done.3 = f32[16,125,512]{2,1,0:T(8,128)} async-done(((f32[16,125,512]{2,1,0:T(8,128)}), f32[16,125,512]{2,1,0:T(8,128)}, u32[]{:S(2)}, u32[]{:S(2)}) %all-to-all-start.3) | async-done | bytes 4096032 | tf_op jit(solution)/shard_map/all_to_all | solution.py:78
  545.0 29.9 %all_to_all.35 = bf16[16,125,512]{2,1,0:T(8,128)(2,1)S(1)} all-to-all(bf16[16,125,512]{2,1,0:T(8,128)(2,1)S(1)} %fusion.37), channel_id=1, replica_groups=mesh['shard'=16,'rep'=8] {'shard'}, dimensions={0} | all-to-all | bytes 4096000 | tf_op jit(solution)/shard_map/all_to_all | solution.py:76
  579.4 14.4 %fusion.24 = f32[40,125,512]{2,1,0:T(8,128)} fusion(bf16[40,512,512]{2,1,0:T(8,128)(2,1)} %bitcast.57, bf16[40,125,512]{2,1,0:T(8,128)(2,1)} %gather_fusion.6, pred[40]{0:T(512)(128)(4,1)S(1)} %copy-done.6), kind=kOutput, calls=%fused_computation.45 | convolution fusion | flops 2624000000 | bytes 36331560 | tf_op jit(solution)/shard_map/pcj,pij->pci/dot_general | solution.py:56
  598.5 15.3 %fusion.22 = f32[40,125,512]{2,1,0:T(8,128)} fusion(bf16[40,512,512]{2,1,0:T(8,128)(2,1)} %bitcast.58, bf16[40,125,512]{2,1,0:T(8,128)(2,1)} %gather_fusion.7, pred[40]{0:T(512)(128)(4,1)S(1)} %get-tuple-element.80), kind=kOutput, calls=%fused_computation.43 | convolution fusion | flops 2624000000 | bytes 36331560 | tf_op jit(solution)/shard_map/pci,pij->pcj/dot_general | solution.py:59
  613.8 16.0 %fusion.14 = f32[16,125,512]{2,0,1:T(8,128)S(1)} fusion(f32[40,125,512]{2,1,0:T(8,128)} %fusion.22, s32[40]{0:T(128)S(1)} %get-tuple-element.71), kind=kOutput, calls=%fused_computation.33 | convolution fusion | flops 491520640 | bytes 14336160 | tf_op jit(solution)/shard_map/pk,pcx->kcx/dot_general | solution.py:63
  629.9 9.8 %fusion.46 = f32[16,125,512]{2,0,1:T(8,128)S(1)} fusion(f32[16,125,512]{2,0,1:T(8,128)S(1)} %fusion.14, f32[40,125,512]{2,1,0:T(8,128)S(1)} %copy-done.2, s32[40]{0:T(128)S(1)} %get-tuple-element.81), kind=kOutput, calls=%fused_computation.65 | convolution fusion | flops 492544640 | bytes 18432160 | tf_op jit(solution)/shard_map/pk,pcx->kcx/dot_general | solution.py:62
  642.4 50.7 %all_to_all.36 = f32[16,125,512]{2,1,0:T(8,128)S(1)} all-to-all(f32[16,125,512]{2,1,0:T(8,128)S(1)} %copy.16), channel_id=1, replica_groups=mesh['shard'=16,'rep'=8] {'shard'}, dimensions={0} | all-to-all | bytes 8192000 | tf_op jit(solution)/shard_map/all_to_all | solution.py:78
  (72 shorter events, 50.0 us)
Async XLA Ops:
  0.0 8.2 %copy-start = (s32[640,2]{0,1:T(2,128)S(1)}, s32[640,2]{0,1:T(2,128)}, u32[]{:S(2)}) copy-start(s32[640,2]{0,1:T(2,128)} %param.14) | copy-start | bytes 15364
  0.0 8.3 %copy-start.7 = (s32[256]{0:T(256)S(1)}, s32[256]{0:T(256)}, u32[]{:S(2)}) copy-start(s32[256]{0:T(256)} %param.15) | copy-start | bytes 3076
  0.0 195.0 %all-to-all-start = ((bf16[16,512,768]{2,1,0:T(8,128)(2,1)}), bf16[16,512,768]{2,1,0:T(8,128)(2,1)}, u32[]{:S(2)}, u32[]{:S(2)}) async-start(bf16[16,512,768]{2,1,0:T(8,128)(2,1)} %param.12), calls=%async_computation | async-start | bytes 25165824 | tf_op jit(solution)/shard_map/all_to_all | solution.py:68
  195.0 176.5 %copy-start.3 = (bf16[16,125,512]{2,0,1:T(8,128)(2,1)S(1)}, bf16[16,125,512]{2,0,1:T(8,128)(2,1)}, u32[]{:S(2)}) copy-start(bf16[16,125,512]{2,0,1:T(8,128)(2,1)} %param.13) | copy-start | bytes 6144004
  374.2 31.1 %all-to-all-start.2 = ((bf16[16,125,512]{2,1,0:T(8,128)(2,1)}), bf16[16,125,512]{2,1,0:T(8,128)(2,1)S(1)}, u32[]{:S(2)}, u32[]{:S(2)}) async-start(bf16[16,125,512]{2,1,0:T(8,128)(2,1)} %fusion.38), calls=%async_computation.2 | async-start | bytes 4194304 | tf_op jit(solution)/shard_map/all_to_all | solution.py:76
  440.6 4.5 copy-start.6
  478.4 62.3 %copy-start.4 = (bf16[16,125,512]{2,0,1:T(8,128)(2,1)S(1)}, bf16[16,125,512]{2,0,1:T(8,128)(2,1)}, u32[]{:S(2)}) copy-start(bf16[16,125,512]{2,0,1:T(8,128)(2,1)} %param.13) | copy-start | bytes 6144004
  478.4 62.3 %all-to-all-start.3 = ((f32[16,125,512]{2,1,0:T(8,128)}), f32[16,125,512]{2,1,0:T(8,128)}, u32[]{:S(2)}, u32[]{:S(2)}) async-start(f32[16,125,512]{2,1,0:T(8,128)} %copy.13), calls=%async_computation.3 | async-start | bytes 8388608 | tf_op jit(solution)/shard_map/all_to_all | solution.py:78
  613.8 16.1 %copy-start.2 = (f32[40,125,512]{2,1,0:T(8,128)S(1)}, f32[40,125,512]{2,1,0:T(8,128)}, u32[]{:S(2)}) copy-start(f32[40,125,512]{2,1,0:T(8,128)} %fusion.24) | copy-start | bytes 30720004
  642.3 50.7 %copy-start.5 = (bf16[16,125,512]{2,0,1:T(8,128)(2,1)S(1)}, bf16[16,125,512]{2,0,1:T(8,128)(2,1)}, u32[]{:S(2)}) copy-start(bf16[16,125,512]{2,0,1:T(8,128)(2,1)} %param.13) | copy-start | bytes 6144004
  693.0 5.9 copy-start.1
where the time goes:
time: 709 us; the launch traced here: 699 us
  waiting for transfers between devices  269 us (38%)
  matrix products  178 us (25%)
  local copies, waits for them, and re-layouts  109 us (15%)
  blocking collectives  92.6 us (13%)
  other arithmetic  32.7 us (5%)
  starting transfers between devices  16.7 us (2%)
    all_to_all x1, waiting for transfers between devices, body(): lax.all_to_all(embeddings, 'shard', split_axis=0, concat_axis=0, tiled=True)  184 us
    dot_general x4, matrix products, one_batch(): jnp.einsum('pid,pjd->pij', rows_a, rows_b, preferred_element_type=jnp.flo...  63 us
    all_to_all x1, waiting for transfers between devices, body(): lax.all_to_all(products, 'shard', split_axis=0, concat_axis=0, tiled=True)  57.4 us
    all_to_all x1, blocking collectives, body(): lax.all_to_all(products, 'shard', split_axis=0, concat_axis=0, tiled=True)  50.7 us
    gather x4, local copies, waits for them, and re-layouts, one_batch(): rows_b = jnp.take(cluster_emb, right_idx, axis=0)  38.7 us
    gather x4, local copies, waits for them, and re-layouts, one_batch(): rows_a = jnp.take(cluster_emb, left_idx, axis=0)  38.6 us
    dot_general x2, matrix products, propagate(): jnp.einsum('pk,pcx->kcx', onehot_b, to_second, precision=lax.Precision.HI...  31.3 us
    dot_general x2, matrix products, propagate(): jnp.einsum('pci,pij->pcj', labels_a, kernel_tiles, preferred_element_type...  30.8 us
  transfers between devices with their start and end apart: 3, of which 3 were waited for; matrix products, arithmetic and copies ran while one was open for 0% of the time, Pallas kernels for 0%

commit v1 on v0

v1 whole, which is shorter than its diff:
```python
import functools
import math

import jax
import jax.numpy as jnp
from jax import lax
from jax.experimental import pallas as pl
from jax.experimental.pallas import tpu as pltpu
from jax.sharding import PartitionSpec as P

ITERS = 2
ALPHA = 0.9

SLOTS = 16
SIDE = 4
PAIRS = 40
ROWS = 512
DIM = 768
CLASSES = 125
PAD = 128
HALF = ROWS // 2
LANES = 128
UNROLL = 4

MESH = pl.DeviceIdType.MESH
NT = (((1,), (1,)), ((), ()))
NN = (((1,), (0,)), ((), ()))
BF = jnp.bfloat16
F32 = jnp.float32


def dot(a, b, dims):
    return lax.dot_general(a, b, dims, preferred_element_type=F32)


def index_table(block_pairs, block_slot):
    group = lax.axis_index("shard")
    pairs = lax.dynamic_slice_in_dim(block_pairs, group * PAIRS, PAIRS, 0)
    slots = lax.dynamic_slice_in_dim(block_slot, group * SLOTS, SLOTS, 0)
    local = (pairs - group * SLOTS).reshape(-1)
    members = jnp.arange(SLOTS, dtype=jnp.int32)
    dest = jnp.sum(jnp.where(local[:, None] == members[None, :], (slots // SLOTS)[None, :], 0), axis=1)
    term = jnp.arange(2 * PAIRS, dtype=jnp.int32)
    before = (dest[:, None] == dest[None, :]) & (term[None, :] < term[:, None])
    prev = jnp.max(jnp.where(before, term[None, :], -1), axis=1)
    prev = jnp.where(prev < 0, 2 * PAIRS, prev)
    last = jnp.max(jnp.where(dest[None, :] == members[:, None], term[None, :], 0), axis=1)
    return jnp.concatenate([dest, prev, last]).astype(jnp.int32)


def main_kernel(
    idx, emb, lab, ret,
    E, K, T, W, LT, SB, L, O, O2, R, SC,
    se, re, sy, ry, sd, rd, sl, rl, sr, rr, loc,
):
    me = lax.axis_index("shard")
    rep = lax.axis_index("rep")
    y, core = rep // 2, rep % 2
    z, x = me // SIDE, me % SIDE
    up = ((y + 1) % SIDE) * 2 + core
    down = ((y + SIDE - 1) % SIDE) * 2 + core
    sibling = y * 2 + (1 - core)
    quarters = (y, (y + 2) % SIDE, (y + 3) % SIDE, (y + 1) % SIDE)

    def dest_of(u):
        return idx[u]

    def prev_of(u):
        return idx[2 * PAIRS + u]

    def last_of(s):
        return idx[4 * PAIRS + s]

    def to(k):
        return ((z + k // SIDE) % SIDE) * SIDE + (x + k % SIDE) % SIDE

    def source(k):
        return ((z + SIDE - k // SIDE) % SIDE) * SIDE + (x + SIDE - k % SIDE) % SIDE

    def remote(src, dst, send, recv, shard, r):
        return pltpu.make_async_remote_copy(
            src, dst, send, recv, device_id={"shard": shard, "rep": r}, device_id_type=MESH
        )

    def emb_copy(k, i):
        q = quarters[i]
        return remote(emb.at[to(k), q, core], E.at[me, q, core], se.at[k, i], re.at[k, i], to(k), rep)

    def y_copy(k, i):
        piece = E.at[source(k), quarters[0], core]
        return remote(piece, piece, sy.at[k, i], ry.at[k, i], me, (up, down)[i])

    def sib_copy(k, i):
        piece = E.at[source(k), quarters[i], core]
        return remote(piece, piece, sd.at[k, i], rd.at[k, i], me, sibling)

    def lab_copy(k):
        return remote(SB.at[to(k)], L.at[me], sl.at[k], rl.at[k], to(k), rep)

    def ret_copy(k, h):
        cols = pl.ds(h * HALF, HALF)
        return remote(
            SB.at[to(k), :, cols], ret.at[me, :, cols], sr.at[k, h], rr.at[k, h], to(k), rep
        )

    def ret_own(h):
        cols = pl.ds(h * HALF, HALF)
        return pltpu.make_async_copy(SB.at[me, :, cols], ret.at[me, :, cols], loc.at[h])

    own_emb = pltpu.make_async_copy(emb.at[me], E.at[me], loc.at[0])
    own_lab = pltpu.make_async_copy(lab, LT, loc.at[1])
    own_emb.start()
    own_lab.start()

    barrier = pltpu.get_barrier_semaphore()

    @pl.loop(1, SLOTS)
    def _(k):
        pl.semaphore_signal(barrier, inc=1, device_id={"shard": to(k), "rep": rep}, device_id_type=MESH)

    for r in (up, down, sibling):
        pl.semaphore_signal(barrier, inc=1, device_id={"shard": me, "rep": r}, device_id_type=MESH)
    pl.semaphore_wait(barrier, SLOTS + 2)

    for i in range(2):
        @pl.loop(1, SLOTS)
        def _(k):
            emb_copy(k, i).start()

    T[2 * PAIRS] = jnp.zeros((PAD, HALF), F32)
    R[2 * PAIRS] = jnp.zeros((1, ROWS), F32)

    own_lab.wait()
    for c in range(ROWS // LANES):
        cols = slice(c * LANES, (c + 1) * LANES)
        b = c % 2
        W[b, 0 : SLOTS * CLASSES, :] = LT[:, cols].astype(F32)
        W[b, SLOTS * CLASSES : SLOTS * PAD, :] = jnp.zeros((SLOTS * (PAD - CLASSES), LANES), F32)
        for s in range(SLOTS):
            SB[s, :, cols] = W[b, pl.ds(s, PAD, stride=SLOTS), :].astype(BF)
    L[me] = SB[me]

    @pl.loop(1, SLOTS)
    def _(k):
        lab_copy(k).start()

    @pl.loop(1, SLOTS)
    def _(k):
        emb_copy(k, 0).wait_recv()
        y_copy(k, 0).start()
        y_copy(k, 1).start()
        sib_copy(k, 0).start()

    @pl.loop(1, SLOTS)
    def _(k):
        y_copy(k, 0).wait_recv()
        y_copy(k, 1).wait_recv()
        sib_copy(k, 2).start()
        sib_copy(k, 3).start()
        emb_copy(k, 1).wait_recv()
        sib_copy(k, 1).start()

    @pl.loop(1, SLOTS)
    def _(k):
        for i in range(4):
            sib_copy(k, i).wait_recv()
    own_emb.wait()

    scale = math.log2(math.e) / math.sqrt(DIM)

    def tile(t):
        a = E[dest_of(2 * t)].reshape(ROWS, DIM)
        b = E[dest_of(2 * t + 1)].reshape(ROWS, DIM)
        kernel = jnp.exp2(dot(a, b, NT) * scale)
        K[t] = kernel.astype(BF)
        cols = jnp.sum(kernel, axis=0, keepdims=True)
        part = kernel[:, 0:128] + kernel[:, 128:256] + kernel[:, 256:384] + kernel[:, 384:512]
        rows = jnp.sum(part.T, axis=0, keepdims=True)
        for u, sums in ((2 * t, rows), (2 * t + 1, cols)):
            R[u] = sums + R[prev_of(u)]

    @pl.loop(0, PAIRS // UNROLL)
    def _(i):
        for j in range(UNROLL):
            tile(i * UNROLL + j)

    @pl.loop(1, SLOTS)
    def _(k):
        lab_copy(k).wait()

    @pl.loop(0, SLOTS)
    def _(s):
        scaling = 1.0 / jnp.sqrt(R[last_of(s)])
        SC[s] = scaling
        O[s] = (L[s].astype(F32) * scaling).astype(BF)

    def products(src, h):
        cols = slice(h * HALF, (h + 1) * HALF)

        def pair(t):
            first, second = dest_of(2 * t), dest_of(2 * t + 1)
            to_first = dot(src[second], K[t, cols, :], NT)
            to_second = dot(src[first], K[t, :, cols], NN)
            for u, product in ((2 * t, to_first), (2 * t + 1, to_second)):
                T[u] = product + T[prev_of(u)]

        @pl.loop(0, PAIRS // UNROLL)
        def _(i):
            for j in range(UNROLL):
                pair(i * UNROLL + j)

    for h in range(2):
        cols = slice(h * HALF, (h + 1) * HALF)
        products(O, h)

        @pl.loop(0, SLOTS)
        def _(s):
            scaling = SC[s, :, cols]
            field = (ALPHA * scaling) * T[last_of(s)] + (1.0 - ALPHA) * L[s, :, cols].astype(F32)
            O2[s, :, cols] = (field * scaling).astype(BF)

    for h in range(2):
        cols = slice(h * HALF, (h + 1) * HALF)
        products(O2, h)

        def finish(s):
            SB[s, :, cols] = ((ALPHA * SC[s, :, cols]) * T[last_of(s)]).astype(BF)

        @pl.loop(1, SLOTS)
        def _(k):
            finish(to(k))
            ret_copy(k, h).start()

        finish(me)
        ret_own(h).start()

    @pl.loop(1, SLOTS)
    def _(k):
        for i in range(2):
            emb_copy(k, i).wait_send()
            y_copy(k, i).wait_send()
        for i in range(4):
            sib_copy(k, i).wait_send()

    for h in range(2):
        @pl.loop(1, SLOTS)
        def _(k):
            ret_copy(k, h).wait()
        ret_own(h).wait()


def finish_kernel(ret, lab, out, W):
    for c in range(ROWS // LANES):
        cols = slice(c * LANES, (c + 1) * LANES)
        for s in range(SLOTS):
            W[c, pl.ds(s, 16, stride=SLOTS), :] = ret[s, :, cols].astype(F32)
        out[:, cols] = W[c] + (1.0 - ALPHA) * lab[:, cols].astype(F32)


def body(embeddings, labels, block_pairs, block_slot):
    idx = index_table(block_pairs, block_slot)
    emb = embeddings.reshape(SLOTS, SIDE, 2, ROWS // (2 * SIDE), DIM)
    lab = jnp.transpose(labels, (1, 0, 2)).reshape(CLASSES * SLOTS, ROWS)
    sems = pltpu.SemaphoreType.DMA
    ret = pl.pallas_call(
        main_kernel,
        out_shape=jax.ShapeDtypeStruct((SLOTS, PAD, ROWS), BF),
        in_specs=[
            pl.BlockSpec(memory_space=pltpu.SMEM),
            pl.BlockSpec(memory_space=pl.ANY),
            pl.BlockSpec(memory_space=pl.ANY),
        ],
        out_specs=pl.BlockSpec(memory_space=pl.ANY),
        scratch_shapes=[
            pltpu.VMEM((SLOTS, SIDE, 2, ROWS // (2 * SIDE), DIM), BF),
            pltpu.VMEM((PAIRS, ROWS, ROWS), BF),
            pltpu.VMEM((2 * PAIRS + 1, PAD, HALF), F32),
            pltpu.VMEM((2, SLOTS * PAD, LANES), F32),
            pltpu.VMEM((SLOTS * CLASSES, ROWS), BF),
            pltpu.VMEM((SLOTS, PAD, ROWS), BF),
            pltpu.VMEM((SLOTS, PAD, ROWS), BF),
            pltpu.VMEM((SLOTS, PAD, ROWS), BF),
            pltpu.VMEM((SLOTS, PAD, ROWS), BF),
            pltpu.VMEM((2 * PAIRS + 1, 1, ROWS), F32),
            pltpu.VMEM((SLOTS, 1, ROWS), F32),
            sems((SLOTS, 2)), sems((SLOTS, 2)),
            sems((SLOTS, 2)), sems((SLOTS, 2)),
            sems((SLOTS, 4)), sems((SLOTS, 4)),
            sems((SLOTS,)), sems((SLOTS,)),
            sems((SLOTS, 2)), sems((SLOTS, 2)),
            sems((2,)),
        ],
        compiler_params=pltpu.CompilerParams(
            vmem_limit_bytes=61 * 2**20, collective_id=0, has_side_effects=True
        ),
    )(idx, emb, lab)
    block = 16 * SLOTS
    out = pl.pallas_call(
        finish_kernel,
        out_shape=jax.ShapeDtypeStruct((CLASSES * SLOTS, ROWS), F32),
        grid=(PAD // 16,),
        in_specs=[
            pl.BlockSpec((SLOTS, 16, ROWS), lambda i: (0, i, 0)),
            pl.BlockSpec((block, ROWS), lambda i: (i, 0)),
        ],
        out_specs=pl.BlockSpec((block, ROWS), lambda i: (i, 0)),
        scratch_shapes=[pltpu.VMEM((ROWS // LANES, block, LANES), F32)],
    )(ret, lab)
    return jnp.transpose(out.reshape(CLASSES, SLOTS, ROWS), (1, 0, 2))


def solution(mesh):
    return jax.shard_map(
        body,
        mesh=mesh,
        in_specs=(P("shard", None, None), P("shard", "rep", None), P(), P()),
        out_specs=P("shard", "rep", None),
        check_vma=False,
    )
```

time: 709 us -> 135 us (0.19); the launches traced: 699 us -> 133 us
  waiting for transfers between devices: 269 us -> 0 us
  matrix products: 178 us -> 0 us
  Pallas kernels: 0 us -> 130 us
  local copies, waits for them, and re-layouts: 109 us -> 0.2 us
  blocking collectives: 92.6 us -> 0 us
  other arithmetic: 32.7 us -> 2.55 us
  starting transfers between devices: 16.7 us -> 0 us
    all_to_all x3 -> x0, waiting for transfers between devices: 269 us -> none  [the longest x1 184 us: body(): lax.all_to_all(embeddings, 'shard', split_axis=0, concat_axis=0, tiled=True)]
    dot_general x14 -> x0, matrix products: 178 us -> none  [the longest x4 63 us: one_batch(): jnp.einsum('pid,pjd->pij', rows_a, rows_b, preferred_element_type=jnp.flo...]
    pallas_call x0 -> x2, Pallas kernels: none -> 130 us  [the longest x1 123 us: body(): pl.pallas_call(main_kernel, out_shape=jax.ShapeDtypeStruct((SLOTS, PAD, R...]
    gather x14 -> x0, local copies, waits for them, and re-layouts: 97.4 us -> none  [the longest x4 38.7 us: one_batch(): rows_b = jnp.take(cluster_emb, right_idx, axis=0)]
    all_to_all x3 -> x0, blocking collectives: 92.6 us -> none  [the longest x1 50.7 us: body(): lax.all_to_all(products, 'shard', split_axis=0, concat_axis=0, tiled=True)]
    reduce_sum x4 -> x1, other arithmetic: 23.4 us -> 0.09 us  [index_table(): jnp.sum(jnp.where(local[:, None] == members[None, :], (slots // SLOTS)[No...]
    all_to_all x3 -> x0, starting transfers between devices: 16.7 us -> none  [the longest x1 8.14 us: body(): lax.all_to_all(embeddings, 'shard', split_axis=0, concat_axis=0, tiled=True)]
    add x3 -> x0, local copies, waits for them, and re-layouts: 11.3 us -> none  [the longest x2 6.97 us: propagate(): summed + jnp.einsum('pk,pcx->kcx', onehot_b, to_second, precision=lax.Pre...]
  transfers between devices with their start and end apart: 3 -> 0, of which waited for: 3 -> 0; matrix products, arithmetic and copies ran while one was open for 0% -> 0% of each run, Pallas kernels for 0% -> 0%
where the time goes in v1:
time: 135 us; the launch traced here: 133 us
  Pallas kernels  130 us (96%)
  other arithmetic  2.55 us (2%)
    pallas_call x1, Pallas kernels, body(): pl.pallas_call(main_kernel, out_shape=jax.ShapeDtypeStruct((SLOTS, PAD, R...  123 us
    pallas_call x1, Pallas kernels, body(): pl.pallas_call(finish_kernel, out_shape=jax.ShapeDtypeStruct((CLASSES * S...  7.32 us

profile of v1, /device:TPU:0, one launch (start us, length us, event | category | flops | bytes accessed | tf_op | source)
XLA Modules:
  0.0 132.9 jit_solution(4547590037359642017)
XLA Ops:
  0.0 0.8 and_select_fusion
  0.8 0.8 dynamic-slice_subtract_fusion
  1.5 0.1 copy.7
  1.6 0.1 eq.20
  1.7 0.1 select_reduce_fusion.2
  1.8 0.1 select_reduce_fusion.1
  1.9 0.2 select_reduce_fusion
  2.1 0.6 pad_add_fusion.idx
  2.8 122.8 %shard_map.46.ret = bf16[16,128,512]{2,1,0:T(8,128)(2,1)} custom-call(s32[176]{0:T(256)} %pad_add_fusion.idx, bf16[16,4,2,64,768]{4,3,2,1,0:T(8,128)(2,1)} %bitcast.7, bf16[2000,512]{1,0:T(8,128)(2,1)} %bitcast.8), custom_call_target="tpu_custom_call" | custom-call | tf_op jit(solution)/shard_map/pallas_call | solution.py:265
  125.5 7.3 %shard_map.47 = f32[2000,512]{1,0:T(8,128)} custom-call(bf16[16,128,512]{2,1,0:T(8,128)(2,1)} %shard_map.46.ret, bf16[2000,512]{1,0:T(8,128)(2,1)} %bitcast.9), custom_call_target="tpu_custom_call" | custom-call | tf_op jit(solution)/shard_map/pallas_call | solution.py:298
  (1 shorter events, 0.0 us)

commit v2 on v1

--- a/solution.py
+++ b/solution.py
@@ -21,6 +21,7 @@
 HALF = ROWS // 2
 LANES = 128
 UNROLL = 4
+LEAD = 13
 
 MESH = pl.DeviceIdType.MESH
 NT = (((1,), (1,)), ((), ()))
@@ -33,25 +34,10 @@
     return lax.dot_general(a, b, dims, preferred_element_type=F32)
 
 
-def index_table(block_pairs, block_slot):
-    group = lax.axis_index("shard")
-    pairs = lax.dynamic_slice_in_dim(block_pairs, group * PAIRS, PAIRS, 0)
-    slots = lax.dynamic_slice_in_dim(block_slot, group * SLOTS, SLOTS, 0)
-    local = (pairs - group * SLOTS).reshape(-1)
-    members = jnp.arange(SLOTS, dtype=jnp.int32)
-    dest = jnp.sum(jnp.where(local[:, None] == members[None, :], (slots // SLOTS)[None, :], 0), axis=1)
-    term = jnp.arange(2 * PAIRS, dtype=jnp.int32)
-    before = (dest[:, None] == dest[None, :]) & (term[None, :] < term[:, None])
-    prev = jnp.max(jnp.where(before, term[None, :], -1), axis=1)
-    prev = jnp.where(prev < 0, 2 * PAIRS, prev)
-    last = jnp.max(jnp.where(dest[None, :] == members[:, None], term[None, :], 0), axis=1)
-    return jnp.concatenate([dest, prev, last]).astype(jnp.int32)
-
-
 def main_kernel(
-    idx, emb, lab, ret,
-    E, K, T, W, LT, SB, L, O, O2, R, SC,
-    se, re, sy, ry, sd, rd, sl, rl, sr, rr, loc,
+    pairs, slots, emb, lab, out,
+    E, K, T, W, LT, SB, L, O, O2, R, SC, idx,
+    se, re, sy, ry, sd, rd, sl, rl, sr, rr, so, loc,
 ):
     me = lax.axis_index("shard")
     rep = lax.axis_index("rep")
@@ -82,6 +68,9 @@
             src, dst, send, recv, device_id={"shard": shard, "rep": r}, device_id_type=MESH
         )
 
+    def landing(g):
+        return LT.at[pl.ds(g * PAD, PAD), :]
+
     def emb_copy(k, i):
         q = quarters[i]
         return remote(emb.at[to(k), q, core], E.at[me, q, core], se.at[k, i], re.at[k, i], to(k), rep)
@@ -100,15 +89,27 @@
     def ret_copy(k, h):
         cols = pl.ds(h * HALF, HALF)
         return remote(
-            SB.at[to(k), :, cols], ret.at[me, :, cols], sr.at[k, h], rr.at[k, h], to(k), rep
+            SB.at[to(k), :, cols], landing(me).at[:, cols], sr.at[k, h], rr.at[k, h], to(k), rep
         )
 
     def ret_own(h):
         cols = pl.ds(h * HALF, HALF)
-        return pltpu.make_async_copy(SB.at[me, :, cols], ret.at[me, :, cols], loc.at[h])
+        return pltpu.make_async_copy(SB.at[me, :, cols], landing(me).at[:, cols], loc.at[h])
+
+    def out_copies(h):
+        cols = pl.ds(h * HALF, HALF)
+        full = SLOTS * CLASSES // PAD
+        rest = SLOTS * CLASSES - full * PAD
+        yield from (
+            pltpu.make_async_copy(O.at[i, :, cols], out.at[pl.ds(i * PAD, PAD), cols], so.at[h, i])
+            for i in range(full)
+        )
+        yield pltpu.make_async_copy(
+            O.at[full, pl.ds(0, rest), cols], out.at[pl.ds(full * PAD, rest), cols], so.at[h, full]
+        )
 
     own_emb = pltpu.make_async_copy(emb.at[me], E.at[me], loc.at[0])
-    own_lab = pltpu.make_async_copy(lab, LT, loc.at[1])
+    own_lab = pltpu.make_async_copy(lab, LT.at[pl.ds(0, SLOTS * CLASSES), :], loc.at[1])
     own_emb.start()
     own_lab.start()
 
@@ -122,43 +123,62 @@
         pl.semaphore_signal(barrier, inc=1, device_id={"shard": me, "rep": r}, device_id_type=MESH)
     pl.semaphore_wait(barrier, SLOTS + 2)
 
-    for i in range(2):
-        @pl.loop(1, SLOTS)
-        def _(k):
-            emb_copy(k, i).start()
+    @pl.loop(1, SLOTS)
+    def _(k):
+        emb_copy(k, 0).start()
+
+    def walk(t, last):
+        for end in range(2):
+            u = 2 * t + end
+            dest = slots[pairs[end, me * PAIRS + t]] // SLOTS
+            idx[u] = dest
+            prev = 2 * PAIRS
+            for s in range(SLOTS):
+                prev = jnp.where(dest == s, last[s], prev)
+            idx[2 * PAIRS + u] = prev
+            last = tuple(jnp.where(dest == s, u, last[s]) for s in range(SLOTS))
+        return last
+
+    last = lax.fori_loop(0, PAIRS, walk, (jnp.int32(2 * PAIRS),) * SLOTS)
+    for s in range(SLOTS):
+        idx[4 * PAIRS + s] = last[s]
 
     T[2 * PAIRS] = jnp.zeros((PAD, HALF), F32)
     R[2 * PAIRS] = jnp.zeros((1, ROWS), F32)
+
+    @pl.loop(1, SLOTS)
+    def _(k):
+        emb_copy(k, 0).wait_recv()
+        y_copy(k, 0).start()
+        y_copy(k, 1).start()
+        sib_copy(k, 0).start()
+        emb_copy(k, 1).start()
 
     own_lab.wait()
     for c in range(ROWS // LANES):
         cols = slice(c * LANES, (c + 1) * LANES)
         b = c % 2
-        W[b, 0 : SLOTS * CLASSES, :] = LT[:, cols].astype(F32)
+        W[b, 0 : SLOTS * CLASSES, :] = LT[0 : SLOTS * CLASSES, cols].astype(F32)
         W[b, SLOTS * CLASSES : SLOTS * PAD, :] = jnp.zeros((SLOTS * (PAD - CLASSES), LANES), F32)
         for s in range(SLOTS):
             SB[s, :, cols] = W[b, pl.ds(s, PAD, stride=SLOTS), :].astype(BF)
     L[me] = SB[me]
 
-    @pl.loop(1, SLOTS)
-    def _(k):
-        lab_copy(k).start()
-
-    @pl.loop(1, SLOTS)
-    def _(k):
-        emb_copy(k, 0).wait_recv()
-        y_copy(k, 0).start()
-        y_copy(k, 1).start()
-        sib_copy(k, 0).start()
-
-    @pl.loop(1, SLOTS)
-    def _(k):
+    def second_half(k):
         y_copy(k, 0).wait_recv()
         y_copy(k, 1).wait_recv()
         sib_copy(k, 2).start()
         sib_copy(k, 3).start()
         emb_copy(k, 1).wait_recv()
         sib_copy(k, 1).start()
+
+    pl.loop(1, LEAD)(second_half)
+
+    @pl.loop(1, SLOTS)
+    def _(k):
+        lab_copy(k).start()
+
+    pl.loop(LEAD, SLOTS)(second_half)
 
     @pl.loop(1, SLOTS)
     def _(k):
@@ -246,26 +266,31 @@
         @pl.loop(1, SLOTS)
         def _(k):
             ret_copy(k, h).wait()
+
         ret_own(h).wait()
-
-
-def finish_kernel(ret, lab, out, W):
-    for c in range(ROWS // LANES):
-        cols = slice(c * LANES, (c + 1) * LANES)
-        for s in range(SLOTS):
-            W[c, pl.ds(s, 16, stride=SLOTS), :] = ret[s, :, cols].astype(F32)
-        out[:, cols] = W[c] + (1.0 - ALPHA) * lab[:, cols].astype(F32)
+        for c in range(2):
+            cols = slice(h * HALF + c * LANES, h * HALF + (c + 1) * LANES)
+            for s in range(SLOTS):
+                W[c, pl.ds(s, PAD, stride=SLOTS), :] = LT[s * PAD : (s + 1) * PAD, cols].astype(F32)
+            for i in range(SLOTS):
+                O[i, :, cols] = W[c, i * PAD : (i + 1) * PAD, :].astype(BF)
+        for copy in out_copies(h):
+            copy.start()
+
+    for h in range(2):
+        for copy in out_copies(h):
+            copy.wait()
 
 
 def body(embeddings, labels, block_pairs, block_slot):
-    idx = index_table(block_pairs, block_slot)
     emb = embeddings.reshape(SLOTS, SIDE, 2, ROWS // (2 * SIDE), DIM)
     lab = jnp.transpose(labels, (1, 0, 2)).reshape(CLASSES * SLOTS, ROWS)
     sems = pltpu.SemaphoreType.DMA
     ret = pl.pallas_call(
         main_kernel,
-        out_shape=jax.ShapeDtypeStruct((SLOTS, PAD, ROWS), BF),
+        out_shape=jax.ShapeDtypeStruct((CLASSES * SLOTS, ROWS), BF),
         in_specs=[
+            pl.BlockSpec(memory_space=pltpu.SMEM),
             pl.BlockSpec(memory_space=pltpu.SMEM),
             pl.BlockSpec(memory_space=pl.ANY),
             pl.BlockSpec(memory_space=pl.ANY),
@@ -276,36 +301,27 @@
             pltpu.VMEM((PAIRS, ROWS, ROWS), BF),
             pltpu.VMEM((2 * PAIRS + 1, PAD, HALF), F32),
             pltpu.VMEM((2, SLOTS * PAD, LANES), F32),
-            pltpu.VMEM((SLOTS * CLASSES, ROWS), BF),
+            pltpu.VMEM((SLOTS * PAD, ROWS), BF),
             pltpu.VMEM((SLOTS, PAD, ROWS), BF),
             pltpu.VMEM((SLOTS, PAD, ROWS), BF),
             pltpu.VMEM((SLOTS, PAD, ROWS), BF),
             pltpu.VMEM((SLOTS, PAD, ROWS), BF),
             pltpu.VMEM((2 * PAIRS + 1, 1, ROWS), F32),
             pltpu.VMEM((SLOTS, 1, ROWS), F32),
+            pltpu.SMEM((4 * PAIRS + SLOTS,), jnp.int32),
             sems((SLOTS, 2)), sems((SLOTS, 2)),
             sems((SLOTS, 2)), sems((SLOTS, 2)),
             sems((SLOTS, 4)), sems((SLOTS, 4)),
             sems((SLOTS,)), sems((SLOTS,)),
             sems((SLOTS, 2)), sems((SLOTS, 2)),
+            sems((2, SLOTS)),
             sems((2,)),
         ],
         compiler_params=pltpu.CompilerParams(
             vmem_limit_bytes=61 * 2**20, collective_id=0, has_side_effects=True
         ),
-    )(idx, emb, lab)
-    block = 16 * SLOTS
-    out = pl.pallas_call(
-        finish_kernel,
-        out_shape=jax.ShapeDtypeStruct((CLASSES * SLOTS, ROWS), F32),
-        grid=(PAD // 16,),
-        in_specs=[
-            pl.BlockSpec((SLOTS, 16, ROWS), lambda i: (0, i, 0)),
-            pl.BlockSpec((block, ROWS), lambda i: (i, 0)),
-        ],
-        out_specs=pl.BlockSpec((block, ROWS), lambda i: (i, 0)),
-        scratch_shapes=[pltpu.VMEM((ROWS // LANES, block, LANES), F32)],
-    )(ret, lab)
+    )(block_pairs.T, block_slot, emb, lab)
+    out = ret.astype(F32) + (1.0 - ALPHA) * lab.astype(F32)
     return jnp.transpose(out.reshape(CLASSES, SLOTS, ROWS), (1, 0, 2))
 
 

time: 135 us -> 133 us (0.985)
  Pallas kernels: 130 us -> 128 us
  other arithmetic: 2.55 us -> 4.14 us
    add x0 -> x1, other arithmetic: none -> 4.14 us  [body(): out = ret.astype(F32) + (1.0 - ALPHA) * lab.astype(F32)]
    pallas_call x2 -> x1, Pallas kernels: 130 us -> 128 us  [body(): pl.pallas_call(main_kernel, out_shape=jax.ShapeDtypeStruct((CLASSES * SLO...]
where the time goes in v2:
time: 133 us; the launch traced here: 132 us
  Pallas kernels  128 us (96%)
  other arithmetic  4.14 us (3%)
    pallas_call x1, Pallas kernels, body(): pl.pallas_call(main_kernel, out_shape=jax.ShapeDtypeStruct((CLASSES * SLO...  128 us
    add x1, other arithmetic, body(): out = ret.astype(F32) + (1.0 - ALPHA) * lab.astype(F32)  4.14 us

profile of v2, /device:TPU:0, one launch (start us, length us, event | category | flops | bytes accessed | tf_op | source)
XLA Modules:
  0.0 131.8 jit_solution(9088459549476628507)
XLA Ops:
  0.0 0.0 copy-start
  0.0 127.7 %shard_map.46 = bf16[2000,512]{1,0:T(8,128)(2,1)} custom-call(s32[2,640]{1,0:T(2,128)} %bitcast.11, s32[256]{0:T(256)} %slots.1, bf16[16,4,2,64,768]{4,3,2,1,0:T(8,128)(2,1)} %bitcast.9, bf16[2000,512]{1,0:T(8,128)(2,1)} %bitcast.10), custom_call_target="tpu_custom_call" | custom-call | tf_op jit(solution)/shard_map/pallas_call | solution.py:289
  127.7 0.0 copy-done
  127.7 4.1 %multiply_add_fusion = f32[2000,512]{1,0:T(8,128)} fusion(bf16[2000,512]{1,0:T(8,128)(2,1)} %shard_map.46, bf16[16,125,512]{2,0,1:T(8,128)(2,1)S(1)} %copy-done), kind=kLoop, calls=%fused_computation | loop fusion | flops 4096000 | bytes 8192000 | tf_op jit(solution)/shard_map/add | solution.py:324
Async XLA Ops:
  0.0 127.7 %copy-start = (bf16[16,125,512]{2,0,1:T(8,128)(2,1)S(1)}, bf16[16,125,512]{2,0,1:T(8,128)(2,1)}, u32[]{:S(2)}) copy-start(bf16[16,125,512]{2,0,1:T(8,128)(2,1)} %param.5) | copy-start | bytes 6144004

commit v3 on v2

--- a/solution.py
+++ b/solution.py
@@ -21,6 +21,8 @@
 HALF = ROWS // 2
 LANES = 128
 UNROLL = 4
+PAIR_UNROLL = 8
+CHUNKS = ROWS // LANES
 LEAD = 13
 
 MESH = pl.DeviceIdType.MESH
@@ -57,11 +59,18 @@
     def last_of(s):
         return idx[4 * PAIRS + s]
 
+    def offset(k):
+        k = (k * 7) % SLOTS
+        dz, dx = k // SIDE, k % SIDE
+        return jnp.where(core == 0, dz, (SIDE - dx) % SIDE), jnp.where(core == 0, dx, (SIDE - dz) % SIDE)
+
     def to(k):
-        return ((z + k // SIDE) % SIDE) * SIDE + (x + k % SIDE) % SIDE
+        dz, dx = offset(k)
+        return ((z + dz) % SIDE) * SIDE + (x + dx) % SIDE
 
     def source(k):
-        return ((z + SIDE - k // SIDE) % SIDE) * SIDE + (x + SIDE - k % SIDE) % SIDE
+        dz, dx = offset(k)
+        return ((z + SIDE - dz) % SIDE) * SIDE + (x + SIDE - dx) % SIDE
 
     def remote(src, dst, send, recv, shard, r):
         return pltpu.make_async_remote_copy(
@@ -87,17 +96,17 @@
         return remote(SB.at[to(k)], L.at[me], sl.at[k], rl.at[k], to(k), rep)
 
     def ret_copy(k, h):
-        cols = pl.ds(h * HALF, HALF)
+        cols = pl.ds(h * LANES, LANES)
         return remote(
             SB.at[to(k), :, cols], landing(me).at[:, cols], sr.at[k, h], rr.at[k, h], to(k), rep
         )
 
     def ret_own(h):
-        cols = pl.ds(h * HALF, HALF)
+        cols = pl.ds(h * LANES, LANES)
         return pltpu.make_async_copy(SB.at[me, :, cols], landing(me).at[:, cols], loc.at[h])
 
     def out_copies(h):
-        cols = pl.ds(h * HALF, HALF)
+        cols = pl.ds(h * LANES, LANES)
         full = SLOTS * CLASSES // PAD
         rest = SLOTS * CLASSES - full * PAD
         yield from (
@@ -126,6 +135,10 @@
     @pl.loop(1, SLOTS)
     def _(k):
         emb_copy(k, 0).start()
+
+    @pl.loop(1, SLOTS)
+    def _(k):
+        emb_copy(k, 1).start()
 
     def walk(t, last):
         for end in range(2):
@@ -146,14 +159,6 @@
     T[2 * PAIRS] = jnp.zeros((PAD, HALF), F32)
     R[2 * PAIRS] = jnp.zeros((1, ROWS), F32)
 
-    @pl.loop(1, SLOTS)
-    def _(k):
-        emb_copy(k, 0).wait_recv()
-        y_copy(k, 0).start()
-        y_copy(k, 1).start()
-        sib_copy(k, 0).start()
-        emb_copy(k, 1).start()
-
     own_lab.wait()
     for c in range(ROWS // LANES):
         cols = slice(c * LANES, (c + 1) * LANES)
@@ -164,6 +169,17 @@
             SB[s, :, cols] = W[b, pl.ds(s, PAD, stride=SLOTS), :].astype(BF)
     L[me] = SB[me]
 
+    @pl.loop(1, SLOTS)
+    def _(k):
+        lab_copy(k).start()
+
+    @pl.loop(1, SLOTS)
+    def _(k):
+        emb_copy(k, 0).wait_recv()
+        y_copy(k, 0).start()
+        y_copy(k, 1).start()
+        sib_copy(k, 0).start()
+
     def second_half(k):
         y_copy(k, 0).wait_recv()
         y_copy(k, 1).wait_recv()
@@ -173,10 +189,6 @@
         sib_copy(k, 1).start()
 
     pl.loop(1, LEAD)(second_half)
-
-    @pl.loop(1, SLOTS)
-    def _(k):
-        lab_copy(k).start()
 
     pl.loop(LEAD, SLOTS)(second_half)
 
@@ -204,34 +216,36 @@
         for j in range(UNROLL):
             tile(i * UNROLL + j)
 
-    @pl.loop(1, SLOTS)
-    def _(k):
-        lab_copy(k).wait()
-
-    @pl.loop(0, SLOTS)
-    def _(s):
+    def scale_labels(s):
         scaling = 1.0 / jnp.sqrt(R[last_of(s)])
         SC[s] = scaling
         O[s] = (L[s].astype(F32) * scaling).astype(BF)
 
-    def products(src, h):
-        cols = slice(h * HALF, (h + 1) * HALF)
+    scale_labels(me)
+
+    @pl.loop(1, SLOTS)
+    def _(k):
+        lab_copy(k).wait()
+        scale_labels(source(k))
+
+    def products(src, start, width):
+        cols = slice(start, start + width)
 
         def pair(t):
             first, second = dest_of(2 * t), dest_of(2 * t + 1)
             to_first = dot(src[second], K[t, cols, :], NT)
             to_second = dot(src[first], K[t, :, cols], NN)
             for u, product in ((2 * t, to_first), (2 * t + 1, to_second)):
-                T[u] = product + T[prev_of(u)]
-
-        @pl.loop(0, PAIRS // UNROLL)
+                T[u, :, 0:width] = product + T[prev_of(u), :, 0:width]
+
+        @pl.loop(0, PAIRS // PAIR_UNROLL)
         def _(i):
-            for j in range(UNROLL):
-                pair(i * UNROLL + j)
+            for j in range(PAIR_UNROLL):
+                pair(i * PAIR_UNROLL + j)
 
     for h in range(2):
         cols = slice(h * HALF, (h + 1) * HALF)
-        products(O, h)
+        products(O, h * HALF, HALF)
 
         @pl.loop(0, SLOTS)
         def _(s):
@@ -239,12 +253,12 @@
             field = (ALPHA * scaling) * T[last_of(s)] + (1.0 - ALPHA) * L[s, :, cols].astype(F32)
             O2[s, :, cols] = (field * scaling).astype(BF)
 
-    for h in range(2):
-        cols = slice(h * HALF, (h + 1) * HALF)
-        products(O2, h)
+    for h in range(CHUNKS):
+        cols = slice(h * LANES, (h + 1) * LANES)
+        products(O2, h * LANES, LANES)
 
         def finish(s):
-            SB[s, :, cols] = ((ALPHA * SC[s, :, cols]) * T[last_of(s)]).astype(BF)
+            SB[s, :, cols] = ((ALPHA * SC[s, :, cols]) * T[last_of(s), :, 0:LANES]).astype(BF)
 
         @pl.loop(1, SLOTS)
         def _(k):
@@ -262,22 +276,22 @@
         for i in range(4):
             sib_copy(k, i).wait_send()
 
-    for h in range(2):
+    for h in range(CHUNKS):
         @pl.loop(1, SLOTS)
         def _(k):
             ret_copy(k, h).wait()
 
         ret_own(h).wait()
-        for c in range(2):
-            cols = slice(h * HALF + c * LANES, h * HALF + (c + 1) * LANES)
-            for s in range(SLOTS):
-                W[c, pl.ds(s, PAD, stride=SLOTS), :] = LT[s * PAD : (s + 1) * PAD, cols].astype(F32)
-            for i in range(SLOTS):
-                O[i, :, cols] = W[c, i * PAD : (i + 1) * PAD, :].astype(BF)
+        cols = slice(h * LANES, (h + 1) * LANES)
+        b = h % 2
+        for s in range(SLOTS):
+            W[b, pl.ds(s, PAD, stride=SLOTS), :] = LT[s * PAD : (s + 1) * PAD, cols].astype(F32)
+        for i in range(SLOTS):
+            O[i, :, cols] = W[b, i * PAD : (i + 1) * PAD, :].astype(BF)
         for copy in out_copies(h):
             copy.start()
 
-    for h in range(2):
+    for h in range(CHUNKS):
         for copy in out_copies(h):
             copy.wait()
 
@@ -313,9 +327,9 @@
             sems((SLOTS, 2)), sems((SLOTS, 2)),
             sems((SLOTS, 4)), sems((SLOTS, 4)),
             sems((SLOTS,)), sems((SLOTS,)),
-            sems((SLOTS, 2)), sems((SLOTS, 2)),
-            sems((2, SLOTS)),
-            sems((2,)),
+            sems((SLOTS, CHUNKS)), sems((SLOTS, CHUNKS)),
+            sems((CHUNKS, SLOTS)),
+            sems((CHUNKS,)),
         ],
         compiler_params=pltpu.CompilerParams(
             vmem_limit_bytes=61 * 2**20, collective_id=0, has_side_effects=True

time: 133 us -> 122 us (0.917)
  Pallas kernels: 128 us -> 117 us
    pallas_call x1, Pallas kernels: 128 us -> 117 us  [body(): pl.pallas_call(main_kernel, out_shape=jax.ShapeDtypeStruct((CLASSES * SLO...]
where the time goes in v3:
time: 122 us; the launch traced here: 121 us
  Pallas kernels  117 us (96%)
  other arithmetic  4.14 us (3%)
    pallas_call x1, Pallas kernels, body(): pl.pallas_call(main_kernel, out_shape=jax.ShapeDtypeStruct((CLASSES * SLO...  117 us
    add x1, other arithmetic, body(): out = ret.astype(F32) + (1.0 - ALPHA) * lab.astype(F32)  4.14 us

profile of v3, /device:TPU:0, one launch (start us, length us, event | category | flops | bytes accessed | tf_op | source)
XLA Modules:
  0.0 120.7 jit_solution(13350280720387994439)
XLA Ops:
  0.0 0.0 copy-start
  0.0 116.5 %shard_map.46 = bf16[2000,512]{1,0:T(8,128)(2,1)} custom-call(s32[2,640]{1,0:T(2,128)} %bitcast.11, s32[256]{0:T(256)} %slots.1, bf16[16,4,2,64,768]{4,3,2,1,0:T(8,128)(2,1)} %bitcast.9, bf16[2000,512]{1,0:T(8,128)(2,1)} %bitcast.10), custom_call_target="tpu_custom_call" | custom-call | tf_op jit(solution)/shard_map/pallas_call | solution.py:303
  116.5 0.0 copy-done
  116.6 4.1 %multiply_add_fusion = f32[2000,512]{1,0:T(8,128)} fusion(bf16[2000,512]{1,0:T(8,128)(2,1)} %shard_map.46, bf16[16,125,512]{2,0,1:T(8,128)(2,1)S(1)} %copy-done), kind=kLoop, calls=%fused_computation | loop fusion | flops 4096000 | bytes 8192000 | tf_op jit(solution)/shard_map/add | solution.py:338
Async XLA Ops:
  0.0 116.5 %copy-start = (bf16[16,125,512]{2,0,1:T(8,128)(2,1)S(1)}, bf16[16,125,512]{2,0,1:T(8,128)(2,1)}, u32[]{:S(2)}) copy-start(bf16[16,125,512]{2,0,1:T(8,128)(2,1)} %param.5) | copy-start | bytes 6144004

commit v4 on v3

--- a/solution.py
+++ b/solution.py
@@ -20,10 +20,9 @@
 PAD = 128
 HALF = ROWS // 2
 LANES = 128
-UNROLL = 4
+UNROLL = 8
 PAIR_UNROLL = 8
 CHUNKS = ROWS // LANES
-LEAD = 13
 
 MESH = pl.DeviceIdType.MESH
 NT = (((1,), (1,)), ((), ()))
@@ -48,7 +47,7 @@
     up = ((y + 1) % SIDE) * 2 + core
     down = ((y + SIDE - 1) % SIDE) * 2 + core
     sibling = y * 2 + (1 - core)
-    quarters = (y, (y + 2) % SIDE, (y + 3) % SIDE, (y + 1) % SIDE)
+    quarters = (y, (y + 2) % SIDE)
 
     def dest_of(u):
         return idx[u]
@@ -88,9 +87,9 @@
         piece = E.at[source(k), quarters[0], core]
         return remote(piece, piece, sy.at[k, i], ry.at[k, i], me, (up, down)[i])
 
-    def sib_copy(k, i):
-        piece = E.at[source(k), quarters[i], core]
-        return remote(piece, piece, sd.at[k, i], rd.at[k, i], me, sibling)
+    def sib_copy(k):
+        piece = E.at[source(k), :, core]
+        return remote(piece, piece, sd.at[k], rd.at[k], me, sibling)
 
     def lab_copy(k):
         return remote(SB.at[to(k)], L.at[me], sl.at[k], rl.at[k], to(k), rep)
@@ -140,6 +139,29 @@
     def _(k):
         emb_copy(k, 1).start()
 
+    T[2 * PAIRS] = jnp.zeros((PAD, HALF), F32)
+    R[2 * PAIRS] = jnp.zeros((1, ROWS), F32)
+
+    @pl.loop(1, SLOTS)
+    def _(k):
+        emb_copy(k, 0).wait_recv()
+        y_copy(k, 0).start()
+        y_copy(k, 1).start()
+
+    own_lab.wait()
+    for c in range(ROWS // LANES):
+        cols = slice(c * LANES, (c + 1) * LANES)
+        b = c % 2
+        W[b, 0 : SLOTS * CLASSES, :] = LT[0 : SLOTS * CLASSES, cols].astype(F32)
+        W[b, SLOTS * CLASSES : SLOTS * PAD, :] = jnp.zeros((SLOTS * (PAD - CLASSES), LANES), F32)
+        for s in range(SLOTS):
+            SB[s, :, cols] = W[b, pl.ds(s, PAD, stride=SLOTS), :].astype(BF)
+    L[me] = SB[me]
+
+    @pl.loop(1, SLOTS)
+    def _(k):
+        lab_copy(k).start()
+
     def walk(t, last):
         for end in range(2):
             u = 2 * t + end
@@ -156,46 +178,17 @@
     for s in range(SLOTS):
         idx[4 * PAIRS + s] = last[s]
 
-    T[2 * PAIRS] = jnp.zeros((PAD, HALF), F32)
-    R[2 * PAIRS] = jnp.zeros((1, ROWS), F32)
-
-    own_lab.wait()
-    for c in range(ROWS // LANES):
-        cols = slice(c * LANES, (c + 1) * LANES)
-        b = c % 2
-        W[b, 0 : SLOTS * CLASSES, :] = LT[0 : SLOTS * CLASSES, cols].astype(F32)
-        W[b, SLOTS * CLASSES : SLOTS * PAD, :] = jnp.zeros((SLOTS * (PAD - CLASSES), LANES), F32)
-        for s in range(SLOTS):
-            SB[s, :, cols] = W[b, pl.ds(s, PAD, stride=SLOTS), :].astype(BF)
-    L[me] = SB[me]
-
-    @pl.loop(1, SLOTS)
-    def _(k):
-        lab_copy(k).start()
-
-    @pl.loop(1, SLOTS)
-    def _(k):
-        emb_copy(k, 0).wait_recv()
-        y_copy(k, 0).start()
-        y_copy(k, 1).start()
-        sib_copy(k, 0).start()
-
     def second_half(k):
         y_copy(k, 0).wait_recv()
         y_copy(k, 1).wait_recv()
-        sib_copy(k, 2).start()
-        sib_copy(k, 3).start()
         emb_copy(k, 1).wait_recv()
-        sib_copy(k, 1).start()
-
-    pl.loop(1, LEAD)(second_half)
-
-    pl.loop(LEAD, SLOTS)(second_half)
-
-    @pl.loop(1, SLOTS)
-    def _(k):
-        for i in range(4):
-            sib_copy(k, i).wait_recv()
+        sib_copy(k).start()
+
+    pl.loop(1, SLOTS)(second_half)
+
+    @pl.loop(1, SLOTS)
+    def _(k):
+        sib_copy(k).wait_recv()
     own_emb.wait()
 
     scale = math.log2(math.e) / math.sqrt(DIM)
@@ -273,8 +266,7 @@
         for i in range(2):
             emb_copy(k, i).wait_send()
             y_copy(k, i).wait_send()
-        for i in range(4):
-            sib_copy(k, i).wait_send()
+        sib_copy(k).wait_send()
 
     for h in range(CHUNKS):
         @pl.loop(1, SLOTS)
@@ -306,8 +298,8 @@
         in_specs=[
             pl.BlockSpec(memory_space=pltpu.SMEM),
             pl.BlockSpec(memory_space=pltpu.SMEM),
-            pl.BlockSpec(memory_space=pl.ANY),
-            pl.BlockSpec(memory_space=pl.ANY),
+            pl.BlockSpec(memory_space=pltpu.HBM),
+            pl.BlockSpec(memory_space=pltpu.HBM),
         ],
         out_specs=pl.BlockSpec(memory_space=pl.ANY),
         scratch_shapes=[
@@ -325,14 +317,14 @@
             pltpu.SMEM((4 * PAIRS + SLOTS,), jnp.int32),
             sems((SLOTS, 2)), sems((SLOTS, 2)),
             sems((SLOTS, 2)), sems((SLOTS, 2)),
-            sems((SLOTS, 4)), sems((SLOTS, 4)),
+            sems((SLOTS,)), sems((SLOTS,)),
             sems((SLOTS,)), sems((SLOTS,)),
             sems((SLOTS, CHUNKS)), sems((SLOTS, CHUNKS)),
             sems((CHUNKS, SLOTS)),
             sems((CHUNKS,)),
         ],
         compiler_params=pltpu.CompilerParams(
-            vmem_limit_bytes=61 * 2**20, collective_id=0, has_side_effects=True
+            vmem_limit_bytes=58 * 2**20, collective_id=0, has_side_effects=True
         ),
     )(block_pairs.T, block_slot, emb, lab)
     out = ret.astype(F32) + (1.0 - ALPHA) * lab.astype(F32)

time: 122 us -> 121 us (level)
  Pallas kernels: 117 us -> 115 us
where the time goes in v4:
time: 121 us; the launch traced here: 120 us
  Pallas kernels  115 us (95%)
  other arithmetic  4.14 us (3%)
    pallas_call x1, Pallas kernels, body(): pl.pallas_call(main_kernel, out_shape=jax.ShapeDtypeStruct((CLASSES * SLO...  115 us
    add x1, other arithmetic, body(): out = ret.astype(F32) + (1.0 - ALPHA) * lab.astype(F32)  4.14 us

profile of v4, /device:TPU:0, one launch (start us, length us, event | category | flops | bytes accessed | tf_op | source)
XLA Modules:
  0.0 119.5 jit_solution(3271574161831321415)
XLA Ops:
  0.0 0.0 copy-start
  0.0 115.4 %shard_map.46 = bf16[2000,512]{1,0:T(8,128)(2,1)} custom-call(s32[2,640]{1,0:T(2,128)} %bitcast.11, s32[256]{0:T(256)} %slots.1, bf16[16,4,2,64,768]{4,3,2,1,0:T(8,128)(2,1)} %bitcast.9, bf16[2000,512]{1,0:T(8,128)(2,1)} %bitcast.10), custom_call_target="tpu_custom_call" | custom-call | tf_op jit(solution)/shard_map/pallas_call | solution.py:295
  115.4 0.0 copy-done
  115.4 4.1 %multiply_add_fusion = f32[2000,512]{1,0:T(8,128)} fusion(bf16[2000,512]{1,0:T(8,128)(2,1)} %shard_map.46, bf16[16,125,512]{2,0,1:T(8,128)(2,1)S(1)} %copy-done), kind=kLoop, calls=%fused_computation | loop fusion | flops 4096000 | bytes 8192000 | tf_op jit(solution)/shard_map/add | solution.py:330
Async XLA Ops:
  0.0 115.4 %copy-start = (bf16[16,125,512]{2,0,1:T(8,128)(2,1)S(1)}, bf16[16,125,512]{2,0,1:T(8,128)(2,1)}, u32[]{:S(2)}) copy-start(bf16[16,125,512]{2,0,1:T(8,128)(2,1)} %param.5) | copy-start | bytes 6144004

commit v5 on v4

--- a/solution.py
+++ b/solution.py
@@ -37,7 +37,7 @@
 
 def main_kernel(
     pairs, slots, emb, lab, out,
-    E, K, T, W, LT, SB, L, O, O2, R, SC, idx,
+    EA, EB, S, K, T, W, LT, SB, L, O, O2, R, SC, idx,
     se, re, sy, ry, sd, rd, sl, rl, sr, rr, so, loc,
 ):
     me = lax.axis_index("shard")
@@ -79,17 +79,24 @@
     def landing(g):
         return LT.at[pl.ds(g * PAD, PAD), :]
 
-    def emb_copy(k, i):
+    halves = (EA, EB)
+
+    def emb_copy(p, k, i):
         q = quarters[i]
-        return remote(emb.at[to(k), q, core], E.at[me, q, core], se.at[k, i], re.at[k, i], to(k), rep)
-
-    def y_copy(k, i):
-        piece = E.at[source(k), quarters[0], core]
-        return remote(piece, piece, sy.at[k, i], ry.at[k, i], me, (up, down)[i])
-
-    def sib_copy(k):
-        piece = E.at[source(k), :, core]
-        return remote(piece, piece, sd.at[k], rd.at[k], me, sibling)
+        return remote(
+            emb.at[to(k), p, q, core], halves[p].at[me, q, core], se.at[p, k, i], re.at[p, k, i], to(k), rep
+        )
+
+    def y_copy(p, k, i):
+        piece = halves[p].at[source(k), y, core]
+        return remote(piece, piece, sy.at[p, k, i], ry.at[p, k, i], me, (up, down)[i])
+
+    def sib_copy(p, k):
+        piece = halves[p].at[source(k), :, core]
+        return remote(piece, piece, sd.at[p, k], rd.at[p, k], me, sibling)
+
+    def own_emb(p):
+        return pltpu.make_async_copy(emb.at[me, p], halves[p].at[me], loc.at[2 * p])
 
     def lab_copy(k):
         return remote(SB.at[to(k)], L.at[me], sl.at[k], rl.at[k], to(k), rep)
@@ -116,9 +123,9 @@
             O.at[full, pl.ds(0, rest), cols], out.at[pl.ds(full * PAD, rest), cols], so.at[h, full]
         )
 
-    own_emb = pltpu.make_async_copy(emb.at[me], E.at[me], loc.at[0])
     own_lab = pltpu.make_async_copy(lab, LT.at[pl.ds(0, SLOTS * CLASSES), :], loc.at[1])
-    own_emb.start()
+    own_emb(0).start()
+    own_emb(1).start()
     own_lab.start()
 
     barrier = pltpu.get_barrier_semaphore()
@@ -131,22 +138,37 @@
         pl.semaphore_signal(barrier, inc=1, device_id={"shard": me, "rep": r}, device_id_type=MESH)
     pl.semaphore_wait(barrier, SLOTS + 2)
 
-    @pl.loop(1, SLOTS)
-    def _(k):
-        emb_copy(k, 0).start()
-
-    @pl.loop(1, SLOTS)
-    def _(k):
-        emb_copy(k, 1).start()
+    for p in range(2):
+        for i in range(2):
+            @pl.loop(1, SLOTS)
+            def _(k):
+                emb_copy(p, k, i).start()
+
+    def forward(p, k):
+        emb_copy(p, k, 0).wait_recv()
+        y_copy(p, k, 0).start()
+        y_copy(p, k, 1).start()
+
+    def share(p):
+        @pl.loop(1, SLOTS)
+        def _(k):
+            y_copy(p, k, 0).wait_recv()
+            y_copy(p, k, 1).wait_recv()
+            emb_copy(p, k, 1).wait_recv()
+            sib_copy(p, k).start()
+
+        @pl.loop(1, SLOTS)
+        def _(k):
+            sib_copy(p, k).wait_recv()
+
+        own_emb(p).wait()
 
     T[2 * PAIRS] = jnp.zeros((PAD, HALF), F32)
     R[2 * PAIRS] = jnp.zeros((1, ROWS), F32)
 
     @pl.loop(1, SLOTS)
     def _(k):
-        emb_copy(k, 0).wait_recv()
-        y_copy(k, 0).start()
-        y_copy(k, 1).start()
+        forward(0, k)
 
     own_lab.wait()
     for c in range(ROWS // LANES):
@@ -178,36 +200,53 @@
     for s in range(SLOTS):
         idx[4 * PAIRS + s] = last[s]
 
-    def second_half(k):
-        y_copy(k, 0).wait_recv()
-        y_copy(k, 1).wait_recv()
-        emb_copy(k, 1).wait_recv()
-        sib_copy(k).start()
-
-    pl.loop(1, SLOTS)(second_half)
-
-    @pl.loop(1, SLOTS)
-    def _(k):
-        sib_copy(k).wait_recv()
-    own_emb.wait()
+    share(0)
 
     scale = math.log2(math.e) / math.sqrt(DIM)
 
-    def tile(t):
-        a = E[dest_of(2 * t)].reshape(ROWS, DIM)
-        b = E[dest_of(2 * t + 1)].reshape(ROWS, DIM)
-        kernel = jnp.exp2(dot(a, b, NT) * scale)
-        K[t] = kernel.astype(BF)
-        cols = jnp.sum(kernel, axis=0, keepdims=True)
-        part = kernel[:, 0:128] + kernel[:, 128:256] + kernel[:, 256:384] + kernel[:, 384:512]
-        rows = jnp.sum(part.T, axis=0, keepdims=True)
-        for u, sums in ((2 * t, rows), (2 * t + 1, cols)):
-            R[u] = sums + R[prev_of(u)]
-
-    @pl.loop(0, PAIRS // UNROLL)
+    def load(ref, u):
+        return ref[dest_of(u)].reshape(HALF, DIM)
+
+    def corner(t):
+        kernel = jnp.exp2(dot(load(EA, 2 * t), load(EA, 2 * t + 1), NT) * scale)
+        K[t, 0:HALF, 0:HALF] = kernel.astype(BF)
+        S[2 * t + 1] = jnp.sum(kernel, axis=0, keepdims=True)
+        S[2 * t] = jnp.sum((kernel[:, 0:128] + kernel[:, 128:256]).T, axis=0, keepdims=True)
+
+    def rest(t):
+        low_a, high_a = load(EA, 2 * t), load(EB, 2 * t)
+        low_b, high_b = load(EA, 2 * t + 1), load(EB, 2 * t + 1)
+        right = jnp.exp2(dot(jnp.concatenate([low_a, high_a], axis=0), high_b, NT) * scale)
+        K[t, :, HALF:ROWS] = right.astype(BF)
+        left = jnp.exp2(dot(high_a, low_b, NT) * scale)
+        K[t, HALF:ROWS, 0:HALF] = left.astype(BF)
+        part = right[:, 0:128] + right[:, 128:256]
+        high_part = part[HALF:ROWS] + left[:, 0:128] + left[:, 128:256]
+        low_rows = jnp.sum(part[0:HALF].T, axis=0, keepdims=True) + S[2 * t]
+        high_rows = jnp.sum(high_part.T, axis=0, keepdims=True)
+        low_cols = jnp.sum(left, axis=0, keepdims=True) + S[2 * t + 1]
+        high_cols = jnp.sum(right, axis=0, keepdims=True)
+        for u, low, high in ((2 * t, low_rows, high_rows), (2 * t + 1, low_cols, high_cols)):
+            prev = prev_of(u)
+            R[u, :, 0:HALF] = low + R[prev, :, 0:HALF]
+            R[u, :, HALF:ROWS] = high + R[prev, :, HALF:ROWS]
+
+    steps = PAIRS // UNROLL
+    share_of_step = (SLOTS - 1) // steps
+
+    @pl.loop(0, steps)
+    def _(i):
+        for j in range(share_of_step):
+            forward(1, 1 + i * share_of_step + j)
+        for j in range(UNROLL):
+            corner(i * UNROLL + j)
+
+    share(1)
+
+    @pl.loop(0, steps)
     def _(i):
         for j in range(UNROLL):
-            tile(i * UNROLL + j)
+            rest(i * UNROLL + j)
 
     def scale_labels(s):
         scaling = 1.0 / jnp.sqrt(R[last_of(s)])
@@ -263,10 +302,11 @@
 
     @pl.loop(1, SLOTS)
     def _(k):
-        for i in range(2):
-            emb_copy(k, i).wait_send()
-            y_copy(k, i).wait_send()
-        sib_copy(k).wait_send()
+        for p in range(2):
+            for i in range(2):
+                emb_copy(p, k, i).wait_send()
+                y_copy(p, k, i).wait_send()
+            sib_copy(p, k).wait_send()
 
     for h in range(CHUNKS):
         @pl.loop(1, SLOTS)
@@ -289,7 +329,7 @@
 
 
 def body(embeddings, labels, block_pairs, block_slot):
-    emb = embeddings.reshape(SLOTS, SIDE, 2, ROWS // (2 * SIDE), DIM)
+    emb = embeddings.reshape(SLOTS, 2, SIDE, 2, HALF // (2 * SIDE), DIM)
     lab = jnp.transpose(labels, (1, 0, 2)).reshape(CLASSES * SLOTS, ROWS)
     sems = pltpu.SemaphoreType.DMA
     ret = pl.pallas_call(
@@ -303,7 +343,9 @@
         ],
         out_specs=pl.BlockSpec(memory_space=pl.ANY),
         scratch_shapes=[
-            pltpu.VMEM((SLOTS, SIDE, 2, ROWS // (2 * SIDE), DIM), BF),
+            pltpu.VMEM((SLOTS, SIDE, 2, HALF // (2 * SIDE), DIM), BF),
+            pltpu.VMEM((SLOTS, SIDE, 2, HALF // (2 * SIDE), DIM), BF),
+            pltpu.VMEM((2 * PAIRS, 1, HALF), F32),
             pltpu.VMEM((PAIRS, ROWS, ROWS), BF),
             pltpu.VMEM((2 * PAIRS + 1, PAD, HALF), F32),
             pltpu.VMEM((2, SLOTS * PAD, LANES), F32),
@@ -315,9 +357,9 @@
             pltpu.VMEM((2 * PAIRS + 1, 1, ROWS), F32),
             pltpu.VMEM((SLOTS, 1, ROWS), F32),
             pltpu.SMEM((4 * PAIRS + SLOTS,), jnp.int32),
-            sems((SLOTS, 2)), sems((SLOTS, 2)),
-            sems((SLOTS, 2)), sems((SLOTS, 2)),
-            sems((SLOTS,)), sems((SLOTS,)),
+            sems((2, SLOTS, 2)), sems((2, SLOTS, 2)),
+            sems((2, SLOTS, 2)), sems((2, SLOTS, 2)),
+            sems((2, SLOTS)), sems((2, SLOTS)),
             sems((SLOTS,)), sems((SLOTS,)),
             sems((SLOTS, CHUNKS)), sems((SLOTS, CHUNKS)),
             sems((CHUNKS, SLOTS)),

time: 121 us -> 120 us (level)
  no operation moved by 1% of the time
where the time goes in v5:
time: 120 us
  Pallas kernels  115 us (96%)
  other arithmetic  4.14 us (3%)
    pallas_call x1, Pallas kernels, body(): pl.pallas_call(main_kernel, out_shape=jax.ShapeDtypeStruct((CLASSES * SLO...  115 us
    add x1, other arithmetic, body(): out = ret.astype(F32) + (1.0 - ALPHA) * lab.astype(F32)  4.14 us

profile of v5, /device:TPU:0, one launch (start us, length us, event | category | flops | bytes accessed | tf_op | source)
XLA Modules:
  0.0 119.6 jit_solution(16557087065889649036)
XLA Ops:
  0.0 0.0 copy-start
  0.0 115.4 %shard_map.46 = bf16[2000,512]{1,0:T(8,128)(2,1)} custom-call(s32[2,640]{1,0:T(2,128)} %bitcast.11, s32[256]{0:T(256)} %slots.1, bf16[16,2,4,2,32,768]{5,4,3,2,1,0:T(8,128)(2,1)} %bitcast.9, bf16[2000,512]{1,0:T(8,128)(2,1)} %bitcast.10), custom_call_target="tpu_custom_call" | custom-call | tf_op jit(solution)/shard_map/pallas_call | solution.py:335
  115.4 0.0 copy-done
  115.4 4.1 %multiply_add_fusion = f32[2000,512]{1,0:T(8,128)} fusion(bf16[2000,512]{1,0:T(8,128)(2,1)} %shard_map.46, bf16[16,125,512]{2,0,1:T(8,128)(2,1)S(1)} %copy-done), kind=kLoop, calls=%fused_computation | loop fusion | flops 4096000 | bytes 8192000 | tf_op jit(solution)/shard_map/add | solution.py:372
Async XLA Ops:
  0.0 115.4 %copy-start = (bf16[16,125,512]{2,0,1:T(8,128)(2,1)S(1)}, bf16[16,125,512]{2,0,1:T(8,128)(2,1)}, u32[]{:S(2)}) copy-start(bf16[16,125,512]{2,0,1:T(8,128)(2,1)} %param.5) | copy-start | bytes 6144004

commit v6 on v5

--- a/solution.py
+++ b/solution.py
@@ -38,7 +38,7 @@
 def main_kernel(
     pairs, slots, emb, lab, out,
     EA, EB, S, K, T, W, LT, SB, L, O, O2, R, SC, idx,
-    se, re, sy, ry, sd, rd, sl, rl, sr, rr, so, loc,
+    se, re, sy, ry, sd, rd, sp, rp, sl, rl, sr, rr, so, loc,
 ):
     me = lax.axis_index("shard")
     rep = lax.axis_index("rep")
@@ -91,6 +91,11 @@
         piece = halves[p].at[source(k), y, core]
         return remote(piece, piece, sy.at[p, k, i], ry.at[p, k, i], me, (up, down)[i])
 
+    def pass_copy(k):
+        q = jnp.where(core == 0, (y + 1) % SIDE, (y + SIDE - 1) % SIDE)
+        piece = EB.at[source(k), q, core]
+        return remote(piece, piece, sp.at[k], rp.at[k], me, jnp.where(core == 0, down, up))
+
     def sib_copy(p, k):
         piece = halves[p].at[source(k), :, core]
         return remote(piece, piece, sd.at[p, k], rd.at[p, k], me, sibling)
@@ -138,11 +143,10 @@
         pl.semaphore_signal(barrier, inc=1, device_id={"shard": me, "rep": r}, device_id_type=MESH)
     pl.semaphore_wait(barrier, SLOTS + 2)
 
-    for p in range(2):
-        for i in range(2):
-            @pl.loop(1, SLOTS)
-            def _(k):
-                emb_copy(p, k, i).start()
+    for p, i in ((0, 0), (0, 1), (1, 0)):
+        @pl.loop(1, SLOTS)
+        def _(k):
+            emb_copy(p, k, i).start()
 
     def forward(p, k):
         emb_copy(p, k, 0).wait_recv()
@@ -154,8 +158,17 @@
         def _(k):
             y_copy(p, k, 0).wait_recv()
             y_copy(p, k, 1).wait_recv()
-            emb_copy(p, k, 1).wait_recv()
-            sib_copy(p, k).start()
+            if p == 0:
+                emb_copy(p, k, 1).wait_recv()
+                sib_copy(p, k).start()
+            else:
+                pass_copy(k).start()
+
+        if p == 1:
+            @pl.loop(1, SLOTS)
+            def _(k):
+                pass_copy(k).wait_recv()
+                sib_copy(p, k).start()
 
         @pl.loop(1, SLOTS)
         def _(k):
@@ -304,9 +317,11 @@
     def _(k):
         for p in range(2):
             for i in range(2):
-                emb_copy(p, k, i).wait_send()
+                if p == 0 or i == 0:
+                    emb_copy(p, k, i).wait_send()
                 y_copy(p, k, i).wait_send()
             sib_copy(p, k).wait_send()
+        pass_copy(k).wait_send()
 
     for h in range(CHUNKS):
         @pl.loop(1, SLOTS)
@@ -361,6 +376,7 @@
             sems((2, SLOTS, 2)), sems((2, SLOTS, 2)),
             sems((2, SLOTS)), sems((2, SLOTS)),
             sems((SLOTS,)), sems((SLOTS,)),
+            sems((SLOTS,)), sems((SLOTS,)),
             sems((SLOTS, CHUNKS)), sems((SLOTS, CHUNKS)),
             sems((CHUNKS, SLOTS)),
             sems((CHUNKS,)),

time: 120 us -> 127 us (1.058)
  Pallas kernels: 115 us -> 122 us
    pallas_call x1, Pallas kernels: 115 us -> 122 us  [body(): pl.pallas_call(main_kernel, out_shape=jax.ShapeDtypeStruct((CLASSES * SLO...]
where the time goes in v6:
time: 127 us
  Pallas kernels  122 us (96%)
  other arithmetic  4.14 us (3%)
    pallas_call x1, Pallas kernels, body(): pl.pallas_call(main_kernel, out_shape=jax.ShapeDtypeStruct((CLASSES * SLO...  122 us
    add x1, other arithmetic, body(): out = ret.astype(F32) + (1.0 - ALPHA) * lab.astype(F32)  4.14 us

profile of v6, /device:TPU:0, one launch (start us, length us, event | category | flops | bytes accessed | tf_op | source)
XLA Modules:
  0.0 126.6 jit_solution(636829513087958163)
XLA Ops:
  0.0 0.0 copy-start
  0.0 122.5 %shard_map.46 = bf16[2000,512]{1,0:T(8,128)(2,1)} custom-call(s32[2,640]{1,0:T(2,128)} %bitcast.11, s32[256]{0:T(256)} %slots.1, bf16[16,2,4,2,32,768]{5,4,3,2,1,0:T(8,128)(2,1)} %bitcast.9, bf16[2000,512]{1,0:T(8,128)(2,1)} %bitcast.10), custom_call_target="tpu_custom_call" | custom-call | tf_op jit(solution)/shard_map/pallas_call | solution.py:350
  122.5 0.0 copy-done
  122.5 4.1 %multiply_add_fusion = f32[2000,512]{1,0:T(8,128)} fusion(bf16[2000,512]{1,0:T(8,128)(2,1)} %shard_map.46, bf16[16,125,512]{2,0,1:T(8,128)(2,1)S(1)} %copy-done), kind=kLoop, calls=%fused_computation | loop fusion | flops 4096000 | bytes 8192000 | tf_op jit(solution)/shard_map/add | solution.py:388
Async XLA Ops:
  0.0 122.5 %copy-start = (bf16[16,125,512]{2,0,1:T(8,128)(2,1)S(1)}, bf16[16,125,512]{2,0,1:T(8,128)(2,1)}, u32[]{:S(2)}) copy-start(bf16[16,125,512]{2,0,1:T(8,128)(2,1)} %param.5) | copy-start | bytes 6144004

commit v7 on v5

--- a/solution.py
+++ b/solution.py
@@ -260,7 +260,7 @@
         lab_copy(k).wait()
         scale_labels(source(k))
 
-    def products(src, start, width):
+    def products(src, start, width, unroll):
         cols = slice(start, start + width)
 
         def pair(t):
@@ -270,14 +270,14 @@
             for u, product in ((2 * t, to_first), (2 * t + 1, to_second)):
                 T[u, :, 0:width] = product + T[prev_of(u), :, 0:width]
 
-        @pl.loop(0, PAIRS // PAIR_UNROLL)
+        @pl.loop(0, PAIRS // unroll)
         def _(i):
-            for j in range(PAIR_UNROLL):
-                pair(i * PAIR_UNROLL + j)
+            for j in range(unroll):
+                pair(i * unroll + j)
 
     for h in range(2):
         cols = slice(h * HALF, (h + 1) * HALF)
-        products(O, h * HALF, HALF)
+        products(O, h * HALF, HALF, 20)
 
         @pl.loop(0, SLOTS)
         def _(s):
@@ -287,7 +287,7 @@
 
     for h in range(CHUNKS):
         cols = slice(h * LANES, (h + 1) * LANES)
-        products(O2, h * LANES, LANES)
+        products(O2, h * LANES, LANES, PAIR_UNROLL)
 
         def finish(s):
             SB[s, :, cols] = ((ALPHA * SC[s, :, cols]) * T[last_of(s), :, 0:LANES]).astype(BF)

time: 120 us -> 119 us (level)
  no operation moved by 1% of the time
where the time goes in v7:
time: 119 us
  Pallas kernels  114 us (96%)
  other arithmetic  4.14 us (3%)
    pallas_call x1, Pallas kernels, body(): pl.pallas_call(main_kernel, out_shape=jax.ShapeDtypeStruct((CLASSES * SLO...  114 us
    add x1, other arithmetic, body(): out = ret.astype(F32) + (1.0 - ALPHA) * lab.astype(F32)  4.14 us

profile of v7, /device:TPU:0, one launch (start us, length us, event | category | flops | bytes accessed | tf_op | source)
XLA Modules:
  0.0 118.6 jit_solution(9934155710579397465)
XLA Ops:
  0.0 0.0 copy-start
  0.0 114.4 %shard_map.46 = bf16[2000,512]{1,0:T(8,128)(2,1)} custom-call(s32[2,640]{1,0:T(2,128)} %bitcast.11, s32[256]{0:T(256)} %slots.1, bf16[16,2,4,2,32,768]{5,4,3,2,1,0:T(8,128)(2,1)} %bitcast.9, bf16[2000,512]{1,0:T(8,128)(2,1)} %bitcast.10), custom_call_target="tpu_custom_call" | custom-call | tf_op jit(solution)/shard_map/pallas_call | solution.py:335
  114.4 0.0 copy-done
  114.4 4.1 %multiply_add_fusion = f32[2000,512]{1,0:T(8,128)} fusion(bf16[2000,512]{1,0:T(8,128)(2,1)} %shard_map.46, bf16[16,125,512]{2,0,1:T(8,128)(2,1)S(1)} %copy-done), kind=kLoop, calls=%fused_computation | loop fusion | flops 4096000 | bytes 8192000 | tf_op jit(solution)/shard_map/add | solution.py:372
Async XLA Ops:
  0.0 114.4 %copy-start = (bf16[16,125,512]{2,0,1:T(8,128)(2,1)S(1)}, bf16[16,125,512]{2,0,1:T(8,128)(2,1)}, u32[]{:S(2)}) copy-start(bf16[16,125,512]{2,0,1:T(8,128)(2,1)} %param.5) | copy-start | bytes 6144004
